TPU v7x, 256 devices: a whole 4x4x8 slice. The times are simulated.
256 devices in a mesh: depth: 8 (over y, core), row: 8 (over x, z_lo), col: 4 (over z_hi).
Axes of the slice: x: 4, y: 4, z: 8 (z_hi: 4, z_lo: 2; z = z_hi * 2 + z_lo), core: 2. Of those that a mesh axis runs over, the one named last changes fastest.
Arguments:
- acts: bfloat16 [5120, 6144], P(('depth', 'col'), 'row'), may hold values from -6 to 6
- w_out: bfloat16 [6144, 12288], P(('depth', 'col'), 'row'), may hold values from -0.078125 to 0.078125
- grad_out: bfloat16 [5120, 12288], P(('depth', 'col'), 'row'), may hold values from -6 to 6
Outputs:
- outputs: bfloat16 [5120, 12288], P(('depth', 'col'), 'row')
- grad_acts: bfloat16 [5120, 6144], P(('depth', 'col'), 'row')
- w_grad: bfloat16 [6144, 12288], P(('depth', 'col'), 'row')
All inputs are finite; a program needn't handle non-finite values.
Results may differ from a plain program's by a relative error of at most 0.019.
Values may be sent and summed in bfloat16 or wider, within the bound.
A program may use at most 128 MiB of HBM per device.

v0:
```python
import jax
import jax.numpy as jnp
from jax import lax
from jax.sharding import PartitionSpec as P


def per_device(acts, w_out, grad_out):
    tok_rows = acts.shape[0]
    whole = lax.all_gather(acts, "row", axis=1, tiled=True)
    k_all = whole.shape[1]
    piece = lax.all_gather(w_out, ("depth", "col"), axis=0, tiled=True)
    out_acc = jnp.dot(whole, piece, preferred_element_type=jnp.float32)
    back_part = lax.dot_general(
        grad_out, piece, (((1,), (1,)), ((), ())), preferred_element_type=jnp.float32
    )
    back_acc = back_part
    out_acc, back_acc = (out_acc, back_acc)
    outputs = out_acc.astype(jnp.bfloat16)
    grad_acts = lax.psum_scatter(
        back_acc.astype(jnp.bfloat16), "row", scatter_dimension=1, tiled=True
    )
    col_count = lax.axis_size("col")
    depth_count = lax.axis_size("depth")
    block_rows = k_all // (depth_count * col_count)
    parted = whole.reshape(tok_rows, depth_count, col_count, block_rows)
    regrouped = lax.all_to_all(parted, "col", split_axis=2, concat_axis=0, tiled=True)
    regrouped = regrouped.reshape(col_count * tok_rows, depth_count * block_rows)
    grads_all = lax.all_gather(grad_out, "col", axis=0, tiled=True)
    w_grad = lax.psum_scatter(
        lax.dot_general(
            regrouped, grads_all, (((0,), (0,)), ((), ())), preferred_element_type=jnp.float32
        ).astype(jnp.bfloat16),
        "depth",
        scatter_dimension=0,
        tiled=True,
    )
    return (outputs, grad_acts, w_grad)


def solution(mesh):
    in_specs = (P(("depth", "col"), "row"), P(("depth", "col"), "row"), P(("depth", "col"), "row"))
    out_specs = (P(("depth", "col"), "row"), P(("depth", "col"), "row"), P(("depth", "col"), "row"))
    return jax.shard_map(
        per_device, mesh=mesh, in_specs=in_specs, out_specs=out_specs, check_vma=False
    )
```

profile of v0, /device:TPU:1, one launch (start us, length us, event | category | flops | bytes accessed | tf_op | source)
XLA Modules:
  0.0 401.5 jit_solution(10885374427654206273)
XLA Ops:
  7.2 0.0 all-gather.4.cloned.1.call-start
  7.2 0.7 all-gather.4.cloned.1.call-update
  7.9 0.0 all-gather.8.cloned.1.call-start
  7.9 0.7 all-gather.8.cloned.1.call-update
  8.6 0.0 all-gather.6.cloned.1.call-start
  8.7 0.7 all-gather.6.cloned.1.call-update
  9.4 0.0 reduce-scatter.5.cloned.1.call-start
  9.4 56.3 %all-gather.4.cloned.1.call-done = bf16[160,6144]{1,0:T(8,128)(2,1)} async-done(((bf16[160,768]{1,0:T(8,128)(2,1)}), bf16[160,6144]{1,0:T(8,128)(2,1)}) %all-gather.4.cloned.1.call-update) | async-done | bytes 1966096 | tf_op jit(solution)/shard_map/all_gather | solution.py:9
  65.7 4.4 %reshape.13 = bf16[160,8,4,192]{3,2,1,0:T(4,128)(2,1)S(1)} reshape(bf16[160,6144]{1,0:T(8,128)(2,1)} %all-gather.4.cloned.1.call-done) | data formatting | bytes 3932160 | tf_op jit(solution)/shard_map/reshape | solution.py:25
  70.1 0.3 copy.6
  70.5 91.9 %all_to_all.15 = bf16[160,8,4,192]{3,1,0,2:T(8,128)(2,1)S(1)} all-to-all(bf16[160,8,4,192]{3,1,0,2:T(8,128)(2,1)S(1)} %copy.6), channel_id=1, replica_groups=mesh['depth'=8,'row'=8,'col'=4] {'col'}, dimensions={2} | all-to-all | bytes 3932160 | tf_op jit(solution)/shard_map/all_to_all | solution.py:26
  162.4 3.2 reshape.14
  165.6 0.0 all-gather.8.cloned.1.call-done
  165.6 8.2 %convolution_convert_fusion = bf16[1536,1536]{1,0:T(8,128)(2,1)} fusion(bf16[640,1536]{1,0:T(8,128)(2,1)} %reshape.14, bf16[640,1536]{1,0:T(8,128)(2,1)} %all-gather.8.cloned.1.call-done), kind=kOutput, calls=%fused_computation | convolution fusion | flops 3022258176 | bytes 8650752 | tf_op jit(solution)/shard_map/dot_general | solution.py:30
  173.8 0.0 copy-start
  173.8 0.0 reduce-scatter.5.cloned.1.call-update
  173.8 0.0 copy-start.1
  173.8 0.0 reduce-scatter.3.cloned.1.call-start
  173.9 112.3 %all-gather.6.cloned.1.call-done = bf16[6144,1536]{1,0:T(8,128)(2,1)} async-done(((bf16[192,1536]{1,0:T(8,128)(2,1)}), bf16[6144,1536]{1,0:T(8,128)(2,1)}) %all-gather.6.cloned.1.call-update) | async-done | bytes 18874384 | tf_op jit(solution)/shard_map/all_gather | solution.py:11
  286.1 0.0 copy-done
  286.1 11.7 %convolution_convert_fusion.1 = bf16[160,6144]{1,0:T(8,128)(2,1)} fusion(bf16[160,1536]{1,0:T(8,128)(2,1)S(1)} %copy-done, bf16[6144,1536]{1,0:T(8,128)(2,1)} %all-gather.6.cloned.1.call-done), kind=kOutput, calls=%fused_computation.1 | convolution fusion | flops 3020881920 | bytes 21331968 | tf_op jit(solution)/shard_map/dot_general | solution.py:13
  297.8 0.0 reduce-scatter.3.cloned.1.call-update
  297.9 0.0 copy-done.1
  297.9 8.9 %convolution_convert_fusion.2 = bf16[160,1536]{1,0:T(8,128)(2,1)} fusion(bf16[160,6144]{1,0:T(8,128)(2,1)S(1)} %copy-done.1, bf16[6144,1536]{1,0:T(8,128)(2,1)} %all-gather.6.cloned.1.call-done), kind=kOutput, calls=%fused_computation.2 | convolution fusion | flops 3020144640 | bytes 21331968 | tf_op jit(solution)/shard_map/dot_general | solution.py:12
  306.8 30.7 %reduce-scatter.5.cloned.1.call-done = bf16[192,1536]{1,0:T(8,128)(2,1)} async-done(((bf16[1536,1536]{1,0:T(8,128)(2,1)}), bf16[192,1536]{1,0:T(8,128)(2,1)}) %reduce-scatter.5.cloned.1.call-update) | async-done | bytes 589840 | tf_op jit(solution)/shard_map/reduce_scatter | solution.py:29
  337.4 57.5 %reduce-scatter.3.cloned.1.call-done = bf16[160,768]{1,0:T(8,128)(2,1)} async-done(((bf16[160,6144]{1,0:T(8,128)(2,1)}), bf16[160,768]{1,0:T(8,128)(2,1)}) %reduce-scatter.3.cloned.1.call-update) | async-done | bytes 245776 | tf_op jit(solution)/shard_map/reduce_scatter | solution.py:19
Async XLA Ops:
  7.2 58.5 %all-gather.4.cloned.1.call-start = ((), (), s32[]{:S(2)}) async-start(), calls=%async_computation.3 | async-start | bytes 2211840 | tf_op jit(solution)/shard_map/all_gather | solution.py:9
  7.9 157.7 %all-gather.8.cloned.1.call-start = ((), (), s32[]{:S(2)}) async-start(), calls=%async_computation.6 | async-start | bytes 2457600 | tf_op jit(solution)/shard_map/all_gather | solution.py:28
  8.6 277.5 %all-gather.6.cloned.1.call-start = ((), (), s32[]{:S(2)}) async-start(), calls=%async_computation.4 | async-start | bytes 19464192 | tf_op jit(solution)/shard_map/all_gather | solution.py:11
  9.4 328.0 %reduce-scatter.5.cloned.1.call-start = ((), (), s32[]{:S(2)}) async-start(), calls=%async_computation.7 | async-start | bytes 5308416 | tf_op jit(solution)/shard_map/reduce_scatter | solution.py:29
  173.8 112.4 %copy-start = (bf16[160,1536]{1,0:T(8,128)(2,1)S(1)}, bf16[160,1536]{1,0:T(8,128)(2,1)}, u32[]{:S(2)}) copy-start(bf16[160,1536]{1,0:T(8,128)(2,1)} %param.5) | copy-start | bytes 1474564
  173.8 124.0 %copy-start.1 = (bf16[160,6144]{1,0:T(8,128)(2,1)S(1)}, bf16[160,6144]{1,0:T(8,128)(2,1)}, u32[]{:S(2)}) copy-start(bf16[160,6144]{1,0:T(8,128)(2,1)} %all-gather.4.cloned.1.call-done) | copy-start | bytes 5898244
  173.8 221.1 %reduce-scatter.3.cloned.1.call-start = ((), (), s32[]{:S(2)}) async-start(), calls=%async_computation.5 | async-start | bytes 2211840 | tf_op jit(solution)/shard_map/reduce_scatter | solution.py:19
Sparse Core Ops, SparseCore 0:
  9.8 55.8 all-gather.3
  67.5 97.9 all-gather.7
  168.1 117.9 all-gather.5
  289.1 48.2 reduce-scatter.4
  340.4 54.4 reduce-scatter.2
where the time goes:
time: 402 us; the launch traced here: 401 us
  waiting for transfers between devices  259 us (64%)
  blocking collectives  91.9 us (23%)
  matrix products  28.8 us (7%)
  between operations  13.8 us (3%)
  local copies, waits for them, and re-layouts  7.98 us (2%)
    all_gather x1, waiting for transfers between devices, per_device(): piece = lax.all_gather(w_out, ('depth', 'col'), axis=0, tiled=True)  112 us
    all_to_all x1, blocking collectives, per_device(): lax.all_to_all(parted, 'col', split_axis=2, concat_axis=0, tiled=True)  91.9 us
    reduce_scatter x1, waiting for transfers between devices, per_device(): lax.psum_scatter(back_acc.astype(jnp.bfloat16), 'row', scatter_dimension=...  57.5 us
    all_gather x1, waiting for transfers between devices, per_device(): whole = lax.all_gather(acts, 'row', axis=1, tiled=True)  56.3 us
    reduce_scatter x1, waiting for transfers between devices, per_device(): lax.psum_scatter(lax.dot_general(regrouped, grads_all, (((0,), (0,)), (()...  30.7 us
    dot_general x1, matrix products, per_device(): lax.dot_general(grad_out, piece, (((1,), (1,)), ((), ())), preferred_elem...  11.7 us
    dot_general x1, matrix products, per_device(): out_acc = jnp.dot(whole, piece, preferred_element_type=jnp.float32)  8.89 us
    dot_general x1, matrix products, per_device(): lax.dot_general(regrouped, grads_all, (((0,), (0,)), ((), ())), preferred...  8.2 us
  transfers between devices with their start and end apart: 5, of which 4 were waited for; matrix products, arithmetic and copies ran while one was open for 9% of the time, Pallas kernels for 0%

commit v1 on v0

v1 whole, which is shorter than its diff:
```python
import jax
import jax.numpy as jnp
from jax import lax
from jax.sharding import PartitionSpec as P


def per_device(acts, w_out, grad_out):
    rows, feats = acts.shape
    cols = lax.axis_size("col")
    piece = feats // cols
    parted = lax.all_to_all(
        acts.reshape(rows, cols, piece), "col", split_axis=1, concat_axis=0, tiled=True
    )
    a = lax.all_gather(parted.reshape(rows * cols, piece), "row", axis=1, tiled=True)
    w = lax.all_gather(w_out, "depth", axis=0, tiled=True)
    g = lax.all_gather(grad_out, "col", axis=0, tiled=True)
    y = jnp.dot(a, w, preferred_element_type=jnp.float32).astype(jnp.bfloat16)
    outputs = lax.psum_scatter(y, "col", scatter_dimension=0, tiled=True)
    ga = lax.dot_general(
        g, w, (((1,), (1,)), ((), ())), preferred_element_type=jnp.float32
    ).astype(jnp.bfloat16)
    ga = lax.psum_scatter(ga, "row", scatter_dimension=1, tiled=True)
    ga = lax.all_to_all(
        ga.reshape(cols, rows, piece), "col", split_axis=0, concat_axis=0, tiled=True
    )
    grad_acts = ga.transpose(1, 0, 2).reshape(rows, feats)
    gw = lax.dot_general(
        a, g, (((0,), (0,)), ((), ())), preferred_element_type=jnp.float32
    ).astype(jnp.bfloat16)
    w_grad = lax.psum_scatter(gw, "depth", scatter_dimension=0, tiled=True)
    return (outputs, grad_acts, w_grad)


def solution(mesh):
    spec = P(("depth", "col"), "row")
    return jax.shard_map(
        per_device, mesh=mesh, in_specs=(spec,) * 3, out_specs=(spec,) * 3, check_vma=False
    )
```

time: 402 us -> 310 us (0.77)
  blocking collectives: 91.9 us -> 35.1 us
  waiting for transfers between devices: 259 us -> 229 us
  matrix products: 28.8 us -> 22.7 us
    all_to_all x1 -> x2, blocking collectives: 91.9 us -> 35.1 us  [the longest x1 19.1 us: per_device(): lax.all_to_all(acts.reshape(rows, cols, piece), 'col', split_axis=1, conc...]
    all_gather x3, waiting for transfers between devices: 169 us -> 117 us  [the longest x1 45.9 us: per_device(): lax.all_gather(parted.reshape(rows * cols, piece), 'row', axis=1, tiled=T...]
    reduce_scatter x2 -> x3, waiting for transfers between devices: 88.2 us -> 111 us  [the longest x1 44.8 us: per_device(): w_grad = lax.psum_scatter(gw, 'depth', scatter_dimension=0, tiled=True)]
    dot_general x3, matrix products: 28.8 us -> 22.7 us  [the longest x1 8.1 us: per_device(): lax.dot_general(g, w, (((1,), (1,)), ((), ())), preferred_element_type=jn...]
    reshape x3 -> x4, local copies, waits for them, and re-layouts: 7.97 us -> 3.12 us  [the longest x2 1.29 us: per_device(): acts.reshape(rows, cols, piece)]
  transfers between devices with their start and end apart: 5 -> 6, of which waited for: 4 -> 6; matrix products, arithmetic and copies ran while one was open for 9% -> 9% of each run, Pallas kernels for 0% -> 0%
where the time goes in v1:
time: 310 us; the launch traced here: 307 us
  waiting for transfers between devices  229 us (74%)
  blocking collectives  35.1 us (11%)
  matrix products  22.7 us (7%)
  between operations  14.1 us (5%)
  local copies, waits for them, and re-layouts  5.96 us (2%)
    all_gather x1, waiting for transfers between devices, per_device(): lax.all_gather(parted.reshape(rows * cols, piece), 'row', axis=1, tiled=T...  45.9 us
    reduce_scatter x1, waiting for transfers between devices, per_device(): w_grad = lax.psum_scatter(gw, 'depth', scatter_dimension=0, tiled=True)  44.8 us
    all_gather x1, waiting for transfers between devices, per_device(): w = lax.all_gather(w_out, 'depth', axis=0, tiled=True)  39.5 us
    reduce_scatter x1, waiting for transfers between devices, per_device(): ga = lax.psum_scatter(ga, 'row', scatter_dimension=1, tiled=True)  38.1 us
    all_gather x1, waiting for transfers between devices, per_device(): g = lax.all_gather(grad_out, 'col', axis=0, tiled=True)  31.1 us
    reduce_scatter x1, waiting for transfers between devices, per_device(): outputs = lax.psum_scatter(y, 'col', scatter_dimension=0, tiled=True)  28.2 us
    all_to_all x1, blocking collectives, per_device(): lax.all_to_all(acts.reshape(rows, cols, piece), 'col', split_axis=1, conc...  19.1 us
    all_to_all x1, blocking collectives, per_device(): lax.all_to_all(ga.reshape(cols, rows, piece), 'col', split_axis=0, concat...  16 us
  transfers between devices with their start and end apart: 6, of which 6 were waited for; matrix products, arithmetic and copies ran while one was open for 9% of the time, Pallas kernels for 0%

profile of v1, /device:TPU:1, one launch (start us, length us, event | category | flops | bytes accessed | tf_op | source)
XLA Modules:
  0.0 307.2 jit_solution(8837422982627617087)
XLA Ops:
  7.2 0.0 all-gather.8.cloned.1.call-start
  7.2 0.7 all-gather.8.cloned.1.call-update
  7.9 0.0 all-gather.6.cloned.1.call-start
  7.9 0.7 all-gather.6.cloned.1.call-update
  8.6 0.0 all-gather.4.cloned.1.call-start
  8.7 1.3 reshape.19
  10.0 19.1 %all_to_all.20 = bf16[160,4,192]{2,0,1:T(8,128)(2,1)S(1)} all-to-all(bf16[160,4,192]{2,0,1:T(8,128)(2,1)S(1)} %copy.12), channel_id=1, replica_groups=mesh['depth'=8,'row'=8,'col'=4] {'col'}, dimensions={1} | all-to-all | bytes 491520 | tf_op jit(solution)/shard_map/all_to_all | solution.py:11
  29.0 0.8 copy.13
  29.9 0.0 all-gather.4.cloned.1.call-update
  29.9 0.0 reduce-scatter.6.cloned.1.call-start
  30.0 31.1 %all-gather.8.cloned.1.call-done = bf16[640,1536]{1,0:T(8,128)(2,1)} async-done(((bf16[160,1536]{1,0:T(8,128)(2,1)}), bf16[640,1536]{1,0:T(8,128)(2,1)}) %all-gather.8.cloned.1.call-update) | async-done | bytes 1966096 | tf_op jit(solution)/shard_map/all_gather | solution.py:16
  61.1 39.5 %all-gather.6.cloned.1.call-done = bf16[1536,1536]{1,0:T(8,128)(2,1)} async-done(((bf16[192,1536]{1,0:T(8,128)(2,1)}), bf16[1536,1536]{1,0:T(8,128)(2,1)}) %all-gather.6.cloned.1.call-update) | async-done | bytes 4718608 | tf_op jit(solution)/shard_map/all_gather | solution.py:15
  100.6 8.1 %convolution_convert_fusion.1 = bf16[640,1536]{0,1:T(8,128)(2,1)} fusion(bf16[640,1536]{1,0:T(8,128)(2,1)} %all-gather.8.cloned.1.call-done, bf16[1536,1536]{1,0:T(8,128)(2,1)} %all-gather.6.cloned.1.call-done), kind=kOutput, calls=%fused_computation.1 | convolution fusion | flops 3020881920 | bytes 8650752 | tf_op jit(solution)/shard_map/dot_general | solution.py:19
  108.7 0.0 reduce-scatter.6.cloned.1.call-update
  108.7 0.0 reduce-scatter.4.cloned.1.call-start
  108.8 45.9 %all-gather.4.cloned.1.call-done = bf16[640,1536]{0,1:T(8,128)(2,1)} async-done(((bf16[640,192]{0,1:T(8,128)(2,1)}), bf16[640,1536]{0,1:T(8,128)(2,1)}) %all-gather.4.cloned.1.call-update) | async-done | bytes 1966096 | tf_op jit(solution)/shard_map/all_gather | solution.py:14
  154.7 7.5 %convolution_convert_fusion.2 = bf16[640,1536]{1,0:T(8,128)(2,1)} fusion(bf16[640,1536]{0,1:T(8,128)(2,1)} %all-gather.4.cloned.1.call-done, bf16[1536,1536]{1,0:T(8,128)(2,1)} %all-gather.6.cloned.1.call-done), kind=kOutput, calls=%fused_computation.2 | convolution fusion | flops 3020881920 | bytes 8650752 | tf_op jit(solution)/shard_map/dot_general | solution.py:17
  162.2 0.0 copy-start
  162.2 0.0 reduce-scatter.4.cloned.1.call-update
  162.2 0.0 reduce-scatter.8.cloned.1.call-start
  162.3 1.5 copy-done
  163.8 7.1 %convolution_convert_fusion = bf16[1536,1536]{1,0:T(8,128)(2,1)} fusion(bf16[640,1536]{0,1:T(8,128)(2,1)} %all-gather.4.cloned.1.call-done, bf16[640,1536]{1,0:T(8,128)(2,1)S(1)} %copy-done), kind=kOutput, calls=%fused_computation | convolution fusion | flops 3022258176 | bytes 8650752 | tf_op jit(solution)/shard_map/dot_general | solution.py:27
  170.8 0.0 reduce-scatter.8.cloned.1.call-update
  170.9 38.1 %reduce-scatter.6.cloned.1.call-done = bf16[640,192]{0,1:T(8,128)(2,1)} async-done(((bf16[640,1536]{0,1:T(8,128)(2,1)}), bf16[640,192]{0,1:T(8,128)(2,1)}) %reduce-scatter.6.cloned.1.call-update) | async-done | bytes 245776 | tf_op jit(solution)/shard_map/reduce_scatter | solution.py:22
  209.0 1.1 copy.14
  210.1 16.0 %all_to_all.21 = bf16[4,160,192]{2,1,0:T(8,128)(2,1)S(1)} all-to-all(bf16[4,160,192]{2,1,0:T(8,128)(2,1)S(1)} %bitcast.14), channel_id=1, replica_groups=mesh['depth'=8,'row'=8,'col'=4] {'col'}, dimensions={0} | all-to-all | bytes 491520 | tf_op jit(solution)/shard_map/all_to_all | solution.py:23
  226.1 0.3 copy.15
  226.4 1.0 reshape.22
  227.3 28.2 %reduce-scatter.4.cloned.1.call-done = bf16[160,1536]{1,0:T(8,128)(2,1)} async-done(((bf16[640,1536]{1,0:T(8,128)(2,1)}), bf16[160,1536]{1,0:T(8,128)(2,1)}) %reduce-scatter.4.cloned.1.call-update) | async-done | bytes 491536 | tf_op jit(solution)/shard_map/reduce_scatter | solution.py:18
  255.6 44.8 %reduce-scatter.8.cloned.1.call-done = bf16[192,1536]{1,0:T(8,128)(2,1)} async-done(((bf16[1536,1536]{1,0:T(8,128)(2,1)}), bf16[192,1536]{1,0:T(8,128)(2,1)}) %reduce-scatter.8.cloned.1.call-update) | async-done | bytes 589840 | tf_op jit(solution)/shard_map/reduce_scatter | solution.py:30
  (1 shorter events, 0.0 us)
Async XLA Ops:
  7.2 53.9 %all-gather.8.cloned.1.call-start = ((), (), s32[]{:S(2)}) async-start(), calls=%async_computation.8 | async-start | bytes 2457600 | tf_op jit(solution)/shard_map/all_gather | solution.py:16
  7.9 92.7 %all-gather.6.cloned.1.call-start = ((), (), s32[]{:S(2)}) async-start(), calls=%async_computation.6 | async-start | bytes 5308416 | tf_op jit(solution)/shard_map/all_gather | solution.py:15
  8.6 146.0 %all-gather.4.cloned.1.call-start = ((), (), s32[]{:S(2)}) async-start(), calls=%async_computation.5 | async-start | bytes 2211840 | tf_op jit(solution)/shard_map/all_gather | solution.py:14
  29.9 179.1 %reduce-scatter.6.cloned.1.call-start = ((), (), s32[]{:S(2)}) async-start(), calls=%async_computation.9 | async-start | bytes 2211840 | tf_op jit(solution)/shard_map/reduce_scatter | solution.py:22
  108.7 146.8 %reduce-scatter.4.cloned.1.call-start = ((), (), s32[]{:S(2)}) async-start(), calls=%async_computation.7 | async-start | bytes 2457600 | tf_op jit(solution)/shard_map/reduce_scatter | solution.py:18
  162.2 1.5 copy-start
  162.2 138.1 %reduce-scatter.8.cloned.1.call-start = ((), (), s32[]{:S(2)}) async-start(), calls=%async_computation.10 | async-start | bytes 5308416 | tf_op jit(solution)/shard_map/reduce_scatter | solution.py:30
Sparse Core Ops, SparseCore 0:
  9.8 51.2 all-gather.7
  62.9 37.6 all-gather.5
  103.0 51.6 all-gather.3
  157.1 51.8 reduce-scatter.5
  212.1 43.3 reduce-scatter.3
  258.7 41.6 reduce-scatter.7

commit v2 on v1

v2 whole, which is shorter than its diff:
```python
import jax
import jax.numpy as jnp
from jax import lax
from jax.experimental import pallas as pl
from jax.experimental.pallas import tpu as pltpu
from jax.sharding import PartitionSpec as P

MESH = pl.DeviceIdType.MESH
BF = jnp.bfloat16
F32 = jnp.float32

M1 = 160
MG = 640
KB = 192
XB = 384
N = 1536
H = 80
NC = 512
NJ = N // NC

S_AM, S_AR, S_AX, S_WY, S_WC, S_G, S_Y, S_GX, S_GM, S_GR, S_CS, S_WS = (
    0, 8, 16, 19, 22, 26, 32, 50, 53, 61, 69, 73,
)
N_SEM = 76


def kernel(
    am_in, ar_in, w_in, g_in,
    y_out, gm_out, gr_out, w_out,
    a4, arb, wb, gb, at4, yp, ysend, yrecv, gs, grecv, sx, srem, fm, fr,
    gw, cs, crecv, ws, wrecv, ss, rs, ls,
):
    d, r, c = lax.axis_index("depth"), lax.axis_index("row"), lax.axis_index("col")
    y, k = d // 2, lax.rem(d, 2)
    x, l = r // 2, lax.rem(r, 2)

    def xdev(i):
        return (d, 2 * lax.rem(x + i, 4) + l, c)

    def ydev(i):
        return (2 * lax.rem(y + i, 4) + k, r, c)

    def zdev(dc, dl):
        return (d, 2 * x + lax.rem(l + dl, 2), lax.rem(c + dc, 4))

    sib = (2 * y + 1 - k, r, c)
    offs = [(dc, dl) for dc in (2, 1, 3, 0) for dl in (0, 1) if (dc, dl) != (0, 0)]

    bar = pltpu.get_barrier_semaphore()
    peers = [zdev(*o) for o in offs] + [xdev(i) for i in (1, 2, 3)]
    peers += [ydev(i) for i in (1, 2, 3)] + [sib]
    for p in peers:
        pl.semaphore_signal(bar, inc=1, device_id=p, device_id_type=MESH)
    pl.semaphore_wait(bar, len(peers))

    pending = []

    def copy(src, dst, sem, dev):
        return pltpu.make_async_remote_copy(
            src, dst, ss.at[sem], rs.at[sem], device_id=dev, device_id_type=MESH
        )

    def send(src, dst, sem, dev):
        cp = copy(src, dst, sem, dev)
        cp.start()
        pending.append(cp)

    def arrived(dst, sem, dev):
        copy(dst, dst, sem, dev).wait_recv()

    def rows(i, size):
        return pl.ds(pl.multiple_of(i * size, 16), size)

    def main_lane(q):
        return pl.ds(pl.multiple_of(q * 256, 128), 128)

    for dc, dl in offs:
        t = lax.rem(c + dc, 4)
        o = 2 * dc + dl
        send(am_in.at[t], a4.at[x, rows(c, M1), main_lane(l)], S_AM + o, zdev(dc, dl))
        send(ar_in.at[t], arb.at[2 * c + l], S_AR + o, zdev(dc, dl))
    h0, h1 = pl.ds(0, H), pl.ds(H, H)

    def grow(block, half):
        return pl.ds(pl.multiple_of(block * M1 + half * H, 16), H)

    send(g_in.at[h0], gb.at[grow(c, 0)], S_G + 0, zdev(1, 0))
    send(g_in.at[h1], gb.at[grow(c, 1)], S_G + 1, zdev(3, 0))
    for i in (2, 1, 3):
        send(w_in, wb.at[rows(d, KB)], S_WY + i - 1, ydev(i))
    send(w_in, wb.at[rows(d, KB)], S_WC + 0, sib)
    send(g_in.at[h1], gb.at[grow(c, 1)], S_G + 2, zdev(1, 0))
    send(g_in.at[h0], gb.at[grow(c, 0)], S_G + 3, zdev(3, 0))

    own = [
        pltpu.make_async_copy(am_in.at[c], a4.at[x, rows(c, M1), main_lane(l)], ls.at[0]),
        pltpu.make_async_copy(ar_in.at[c], arb.at[2 * c + l], ls.at[1]),
        pltpu.make_async_copy(w_in, wb.at[rows(d, KB)], ls.at[2]),
        pltpu.make_async_copy(g_in, gb.at[rows(c, M1)], ls.at[3]),
    ]
    for cp in own:
        cp.start()
    own[0].wait()
    own[1].wait()

    for dc, dl in offs:
        cc, ll = lax.rem(c + 4 - dc, 4), lax.rem(l + dl, 2)
        o = 2 * dc + dl
        arrived(a4.at[x, rows(cc, M1), main_lane(ll)], S_AM + o, zdev(dc, dl))
        arrived(arb.at[2 * cc + ll], S_AR + o, zdev(dc, dl))
    lane = lax.broadcasted_iota(jnp.int32, (H, 128), 1)
    left = lane < 64
    for q in range(4):
        p0, p1 = arb[2 * q].astype(F32), arb[2 * q + 1].astype(F32)
        low = jnp.where(left, p0, p1)
        high = pltpu.roll(jnp.where(left, p1, p0), 64, 1)
        a4[x, pl.ds(q * M1, H), pl.ds(128, 128)] = low.astype(BF)
        a4[x, pl.ds(q * M1 + H, H), pl.ds(128, 128)] = high.astype(BF)
    for i in (2, 1, 3):
        send(a4.at[x], a4.at[x], S_AX + i - 1, xdev(i))

    cl, cr, co = lax.rem(c + 3, 4), lax.rem(c + 1, 4), lax.rem(c + 2, 4)
    arrived(gb.at[grow(cl, 0)], S_G + 0, zdev(1, 0))
    send(gb.at[grow(cl, 0)], gb.at[grow(cl, 0)], S_G + 4, zdev(1, 0))
    arrived(gb.at[grow(cr, 1)], S_G + 1, zdev(3, 0))
    send(gb.at[grow(cr, 1)], gb.at[grow(cr, 1)], S_G + 5, zdev(3, 0))

    own[2].wait()
    own[3].wait()
    for i in (1, 3, 2):
        src = 2 * lax.rem(y + 4 - i, 4) + k
        arrived(wb.at[rows(src, KB)], S_WY + i - 1, ydev(i))
        send(wb.at[rows(src, KB)], wb.at[rows(src, KB)], S_WC + i, sib)

    for i in (1, 3, 2):
        src = lax.rem(x + 4 - i, 4)
        arrived(a4.at[src], S_AX + i - 1, xdev(i))
    for i in (0, 1, 3, 2):
        src = 2 * lax.rem(y + 4 - i, 4) + 1 - k
        arrived(wb.at[rows(src, KB)], S_WC + i, sib)

    def yrow(block, half):
        return pl.ds(pl.multiple_of(block * M1 + half * H, 16), H)

    for j in range(NJ):
        @pl.loop(0, NC // 256)
        def _(t):
            cols = pl.ds(pl.multiple_of(j * NC + t * 256, 256), 256)
            a = jnp.concatenate([a4[0], a4[1], a4[2], a4[3]], axis=1)
            yp[:, cols] = jnp.dot(a, wb[:, cols], preferred_element_type=F32)

        cols = pl.ds(j * NC, NC)
        for kind, block, half, dc in ((0, co, 0, 1), (1, co, 1, 3), (2, cr, 1, 1), (3, cl, 0, 3)):
            ysend[kind, j] = yp[yrow(block, half), cols].astype(BF)
            send(ysend.at[kind, j], yrecv.at[kind, j], S_Y + 3 * kind + j, zdev(dc, 0))

    for q in range(4):
        at4[q] = a4[q].T

    arrived(gb.at[grow(cl, 1)], S_G + 2, zdev(1, 0))
    arrived(gb.at[grow(cr, 0)], S_G + 3, zdev(3, 0))
    arrived(gb.at[grow(co, 0)], S_G + 4, zdev(1, 0))
    arrived(gb.at[grow(co, 1)], S_G + 5, zdev(3, 0))

    def nt_dot(a, b):
        return lax.dot_general(a, b, (((1,), (1,)), ((), ())), preferred_element_type=F32)

    for pair in ((2, 1), (3, 0)):
        xa, xb = lax.rem(x + pair[0], 4), lax.rem(x + pair[1], 4)
        wa = pl.multiple_of(xa * XB, 128)
        wc = pl.multiple_of(xb * XB, 128)
        g = gb[...]
        gs[pair[0], :, 0:256] = nt_dot(g, wb[pl.ds(wa, 256), :]).astype(BF)
        mid = jnp.concatenate([wb[pl.ds(wa + 256, 128), :], wb[pl.ds(wc, 128), :]], axis=0)
        mid = nt_dot(g, mid).astype(BF)
        gs[pair[0], :, 256:384] = mid[:, :128]
        gs[pair[1], :, 0:128] = mid[:, 128:]
        gs[pair[1], :, 128:384] = nt_dot(g, wb[pl.ds(wc + 128, 256), :]).astype(BF)
        for i in pair:
            if i:
                send(gs.at[i], grecv.at[i - 1], S_GX + i - 1, xdev(i))

    def relay():
        for j in range(NJ):
            cols = pl.ds(j * NC, NC)
            arrived(yrecv.at[0, j], S_Y + j, zdev(1, 0))
            ysend[4, j] = (yp[yrow(cr, 0), cols] + yrecv[0, j].astype(F32)).astype(BF)
            send(ysend.at[4, j], yrecv.at[4, j], S_Y + 12 + j, zdev(1, 0))
            arrived(yrecv.at[1, j], S_Y + 3 + j, zdev(3, 0))
            ysend[5, j] = (yp[yrow(cl, 1), cols] + yrecv[1, j].astype(F32)).astype(BF)
            send(ysend.at[5, j], yrecv.at[5, j], S_Y + 15 + j, zdev(3, 0))

    relay()

    for pair in ((2, 1), (3, 0)):
        ya, yb = lax.rem(y + pair[0], 4), lax.rem(y + pair[1], 4)

        @pl.loop(0, N // 256)
        def _(t):
            cols = pl.ds(pl.multiple_of(t * 256, 256), 256)
            at = jnp.concatenate([at4[ya], at4[yb]], axis=0)
            acc = jnp.dot(at, gb[:, cols], preferred_element_type=F32)
            for q in range(4):
                gw[2 * pair[q // 2] + q % 2, :, cols] = acc[q * KB : (q + 1) * KB]

        for i in pair:
            cs[i] = gw[2 * i + 1 - k].astype(BF)
            send(cs.at[i], crecv.at[i], S_CS + i, sib)

    for i in (2, 1, 3):
        arrived(crecv.at[i], S_CS + i, sib)
        ws[i - 1] = (gw[2 * i + k] + crecv[i].astype(F32)).astype(BF)
        send(ws.at[i - 1], wrecv.at[i - 1], S_WS + i - 1, ydev(i))
    arrived(crecv.at[0], S_CS + 0, sib)

    for i in (1, 3, 2):
        arrived(grecv.at[i - 1], S_GX + i - 1, xdev(i))
    total = gs[0].astype(F32) + grecv[0].astype(F32)
    total += grecv[1].astype(F32) + grecv[2].astype(F32)
    sx[...] = total.astype(BF)
    for q in range(4):
        t0 = sx[pl.ds(q * M1, H), pl.ds(128, 128)].astype(F32)
        t1 = pltpu.roll(sx[pl.ds(q * M1 + H, H), pl.ds(128, 128)].astype(F32), 64, 1)
        srem[2 * q] = jnp.where(left, t0, t1).astype(BF)
        srem[2 * q + 1] = jnp.where(left, t1, t0).astype(BF)
    for dc, dl in offs:
        cc, ll = lax.rem(c + dc, 4), lax.rem(l + dl, 2)
        o = 2 * dc + dl
        send(sx.at[rows(cc, M1), main_lane(ll)], fm.at[2 * c + l], S_GM + o, zdev(dc, dl))
        send(srem.at[2 * cc + ll], fr.at[2 * c + l], S_GR + o, zdev(dc, dl))
    fm[2 * c + l] = sx[rows(c, M1), main_lane(l)]
    fr[2 * c + l] = srem[2 * c + l]

    for j in range(NJ):
        cols = pl.ds(j * NC, NC)
        for kind, dc in ((2, 1), (3, 3), (4, 1), (5, 3)):
            arrived(yrecv.at[kind, j], S_Y + 3 * kind + j, zdev(dc, 0))
        y_out[h0, cols] = (
            yp[yrow(c, 0), cols] + yrecv[4, j].astype(F32) + yrecv[3, j].astype(F32)
        ).astype(BF)
        y_out[h1, cols] = (
            yp[yrow(c, 1), cols] + yrecv[5, j].astype(F32) + yrecv[2, j].astype(F32)
        ).astype(BF)

    for i in (1, 3, 2):
        arrived(wrecv.at[i - 1], S_WS + i - 1, ydev(i))
    w_out[...] = (
        gw[k] + crecv[0].astype(F32)
        + wrecv[0].astype(F32) + wrecv[1].astype(F32) + wrecv[2].astype(F32)
    ).astype(BF)

    for dc, dl in offs:
        cc, ll = lax.rem(c + 4 - dc, 4), lax.rem(l + dl, 2)
        o = 2 * dc + dl
        arrived(fm.at[2 * cc + ll], S_GM + o, zdev(dc, dl))
        arrived(fr.at[2 * cc + ll], S_GR + o, zdev(dc, dl))
    for q in range(4):
        gm_out[q] = (fm[2 * q].astype(F32) + fm[2 * q + 1].astype(F32)).astype(BF)
        gr_out[q] = (fr[2 * q].astype(F32) + fr[2 * q + 1].astype(F32)).astype(BF)

    for cp in pending:
        cp.wait_send()


def per_device(acts, w_out, grad_out):
    odd = lax.rem(lax.axis_index("row"), 2) == 1
    a3 = acts.reshape(M1, 4, KB).transpose(1, 0, 2)
    main = jnp.where(odd, a3[:, :, 64:], a3[:, :, :128])
    rem = jnp.where(odd, a3[:, :, :64], a3[:, :, 128:])
    top, low = rem[:, :H], rem[:, H:]
    rem = jnp.where(
        odd, jnp.concatenate([low, top], axis=-1), jnp.concatenate([top, low], axis=-1)
    )

    def vm(shape, dtype=BF):
        return pltpu.VMEM(shape, dtype)

    outputs, gm, gr, w_grad = pl.pallas_call(
        kernel,
        out_shape=[
            jax.ShapeDtypeStruct((M1, N), BF),
            jax.ShapeDtypeStruct((4, M1, 128), BF),
            jax.ShapeDtypeStruct((4, H, 128), BF),
            jax.ShapeDtypeStruct((KB, N), BF),
        ],
        in_specs=[pl.BlockSpec(memory_space=pltpu.VMEM)] * 4,
        out_specs=[pl.BlockSpec(memory_space=pltpu.VMEM)] * 4,
        scratch_shapes=[
            vm((4, MG, XB)),
            vm((8, H, 128)),
            vm((N, N)),
            vm((MG, N)),
            vm((4, XB, MG)),
            vm((MG, N), F32),
            vm((6, NJ, H, NC)),
            vm((6, NJ, H, NC)),
            vm((4, MG, XB)),
            vm((3, MG, XB)),
            vm((MG, XB)),
            vm((8, H, 128)),
            vm((8, M1, 128)),
            vm((8, H, 128)),
            vm((8, KB, N), F32),
            vm((4, KB, N)),
            vm((4, KB, N)),
            vm((3, KB, N)),
            vm((3, KB, N)),
            pltpu.SemaphoreType.DMA((N_SEM,)),
            pltpu.SemaphoreType.DMA((N_SEM,)),
            pltpu.SemaphoreType.DMA((4,)),
        ],
        compiler_params=pltpu.CompilerParams(
            collective_id=0, has_side_effects=True, vmem_limit_bytes=60 * 2**20
        ),
        cost_estimate=pl.CostEstimate(
            flops=6 * MG * N * N, bytes_accessed=3 * 2**20, transcendentals=0
        ),
    )(main, rem, w_out, grad_out)

    a, b = gr[:, :, :64], gr[:, :, 64:]
    rem = jnp.where(odd, jnp.concatenate([b, a], axis=1), jnp.concatenate([a, b], axis=1))
    a3 = jnp.where(
        odd, jnp.concatenate([rem, gm], axis=-1), jnp.concatenate([gm, rem], axis=-1)
    )
    grad_acts = a3.transpose(1, 0, 2).reshape(M1, 4 * KB)
    return outputs, grad_acts, w_grad


def solution(mesh):
    spec = P(("depth", "col"), "row")
    return jax.shard_map(
        per_device, mesh=mesh, in_specs=(spec,) * 3, out_specs=(spec,) * 3, check_vma=False
    )
```

time: 310 us -> 125 us (0.40)
  waiting for transfers between devices: 229 us -> 0 us
  Pallas kernels: 0 us -> 115 us
  blocking collectives: 35.1 us -> 0 us
  matrix products: 22.7 us -> 0 us
  between operations: 14.1 us -> 0.71 us
    all_gather x3 -> x0, waiting for transfers between devices: 117 us -> none  [the longest x1 45.9 us: per_device(): lax.all_gather(parted.reshape(rows * cols, piece), 'row', axis=1, tiled=T...]
    pallas_call x0 -> x1, Pallas kernels: none -> 115 us  [per_device(): pl.pallas_call(kernel, out_shape=[jax.ShapeDtypeStruct((M1, N), BF), jax....]
    reduce_scatter x3 -> x0, waiting for transfers between devices: 111 us -> none  [the longest x1 44.8 us: per_device(): w_grad = lax.psum_scatter(gw, 'depth', scatter_dimension=0, tiled=True)]
    all_to_all x2 -> x0, blocking collectives: 35.1 us -> none  [the longest x1 19.1 us: per_device(): lax.all_to_all(acts.reshape(rows, cols, piece), 'col', split_axis=1, conc...]
    dot_general x3 -> x0, matrix products: 22.7 us -> none  [the longest x1 8.1 us: per_device(): lax.dot_general(g, w, (((1,), (1,)), ((), ())), preferred_element_type=jn...]
  transfers between devices with their start and end apart: 6 -> 0, of which waited for: 6 -> 0; matrix products, arithmetic and copies ran while one was open for 9% -> 0% of each run, Pallas kernels for 0% -> 0%
where the time goes in v2:
time: 125 us; the launch traced here: 124 us
  Pallas kernels  115 us (92%)
  local copies, waits for them, and re-layouts  6.51 us (5%)
  other arithmetic  1.82 us (1%)
    pallas_call x1, Pallas kernels, per_device(): pl.pallas_call(kernel, out_shape=[jax.ShapeDtypeStruct((M1, N), BF), jax....  115 us
    unnamed x8, local copies, waits for them, and re-layouts  2.91 us

profile of v2, /device:TPU:1, one launch (start us, length us, event | category | flops | bytes accessed | tf_op | source)
XLA Modules:
  0.0 124.4 jit_solution(13628736353765064736)
XLA Ops:
  0.6 1.3 %reshape.12 = bf16[160,4,192]{2,1,0:T(4,128)(2,1)S(1)} reshape(bf16[160,768]{1,0:T(8,128)(2,1)} %param.3) | data formatting | bytes 491520 | tf_op jit(solution)/shard_map/reshape | solution.py:267
  1.9 0.8 slice_select_fusion.1.am_in
  2.8 0.8 maximum_select_fusion.2.ar_in
  3.5 115.3 %shard_map.58 = (bf16[160,1536]{1,0:T(8,128)(2,1)}, bf16[4,160,128]{2,1,0:T(8,128)(2,1)}, bf16[4,80,128]{2,1,0:T(8,128)(2,1)}, bf16[192,1536]{1,0:T(8,128)(2,1)}) custom-call(bf16[4,160,128]{2,1,0:T(8,128)(2,1)} %slice_select_fusion.1.am_in, bf16[4,80,128]{2,1,0:T(8,128)(2,1)} %maximum_select_fusion.2.ar_in, bf16[192,1536]{1,0:T(8,128)(2,1)} %w_in.1, ...), custom_call_target="tpu_custom_call" | custom-call | flops 9059696640 | bytes 3145728 | tf_op jit(solution)/shard_map/pallas_call | solution.py:278
  118.8 1.1 fusion.2
  119.9 0.0 copy-start.2
  120.0 0.8 copy-done.2
  120.8 0.2 fusion
  121.0 0.0 copy-start.1
  121.0 0.3 copy.7
  121.3 1.0 reshape.13
  122.3 0.0 copy-done.1
  122.3 0.0 copy-start
  122.3 0.8 copy.12
  123.1 0.5 copy-done
  123.5 0.8 copy.13
  (4 shorter events, 0.1 us)
Async XLA Ops:
  119.9 0.9 copy-start.2
  121.0 1.3 %copy-start.1 = (bf16[160,1536]{1,0:T(8,128)(2,1)S(1)}, bf16[160,1536]{1,0:T(8,128)(2,1)}, u32[]{:S(2)}) copy-start(bf16[160,1536]{1,0:T(8,128)(2,1)} %get-tuple-element.18) | copy-start | bytes 1474564
  122.3 1.2 copy-start

commit v3 on v2

--- a/solution.py
+++ b/solution.py
@@ -25,9 +25,9 @@
 
 
 def kernel(
-    am_in, ar_in, w_in, g_in,
-    y_out, gm_out, gr_out, w_out,
-    a4, arb, wb, gb, at4, yp, ysend, yrecv, gs, grecv, sx, srem, fm, fr,
+    acts, w_in, g_in,
+    y_out, ga_out, w_out,
+    am_in, ar_in, a4, arb, wb, gb, at4, yp, ysend, yrecv, gs, grecv, sx, srem, fm, fr,
     gw, cs, crecv, ws, wrecv, ss, rs, ls,
 ):
     d, r, c = lax.axis_index("depth"), lax.axis_index("row"), lax.axis_index("col")
@@ -73,6 +73,36 @@
 
     def main_lane(q):
         return pl.ds(pl.multiple_of(q * 256, 128), 128)
+
+    lane = lax.broadcasted_iota(jnp.int32, (M1, 128), 1)
+    left = lane < 64
+    left_h = left[:H]
+
+    def swap(v):
+        return pltpu.roll(v, 64, 1)
+
+    def pack(lv):
+        def tile(q):
+            return acts[:, 128 * q : 128 * q + 128].astype(F32)
+
+        for t in range(4):
+            q, odd = divmod(KB * t + 64 * lv, 128)
+            if odd:
+                am_in[t] = swap(jnp.where(left, tile(q + 1), tile(q))).astype(BF)
+            else:
+                am_in[t] = acts[:, 128 * q : 128 * q + 128]
+            q, odd = divmod(KB * t + 128 * (1 - lv), 128)
+            first, second = tile(q)[:H], tile(q)[H:]
+            if lv:
+                first, second = second, first
+            if odd:
+                first = swap(first)
+            else:
+                second = swap(second)
+            ar_in[t] = jnp.where(left_h, first, second).astype(BF)
+
+    for lv in (0, 1):
+        pl.when(l == lv)(lambda lv=lv: pack(lv))
 
     for dc, dl in offs:
         t = lax.rem(c + dc, 4)
@@ -108,12 +138,10 @@
         o = 2 * dc + dl
         arrived(a4.at[x, rows(cc, M1), main_lane(ll)], S_AM + o, zdev(dc, dl))
         arrived(arb.at[2 * cc + ll], S_AR + o, zdev(dc, dl))
-    lane = lax.broadcasted_iota(jnp.int32, (H, 128), 1)
-    left = lane < 64
     for q in range(4):
         p0, p1 = arb[2 * q].astype(F32), arb[2 * q + 1].astype(F32)
-        low = jnp.where(left, p0, p1)
-        high = pltpu.roll(jnp.where(left, p1, p0), 64, 1)
+        low = jnp.where(left_h, p0, p1)
+        high = swap(jnp.where(left_h, p1, p0))
         a4[x, pl.ds(q * M1, H), pl.ds(128, 128)] = low.astype(BF)
         a4[x, pl.ds(q * M1 + H, H), pl.ds(128, 128)] = high.astype(BF)
     for i in (2, 1, 3):
@@ -180,17 +208,14 @@
             if i:
                 send(gs.at[i], grecv.at[i - 1], S_GX + i - 1, xdev(i))
 
-    def relay():
-        for j in range(NJ):
-            cols = pl.ds(j * NC, NC)
-            arrived(yrecv.at[0, j], S_Y + j, zdev(1, 0))
-            ysend[4, j] = (yp[yrow(cr, 0), cols] + yrecv[0, j].astype(F32)).astype(BF)
-            send(ysend.at[4, j], yrecv.at[4, j], S_Y + 12 + j, zdev(1, 0))
-            arrived(yrecv.at[1, j], S_Y + 3 + j, zdev(3, 0))
-            ysend[5, j] = (yp[yrow(cl, 1), cols] + yrecv[1, j].astype(F32)).astype(BF)
-            send(ysend.at[5, j], yrecv.at[5, j], S_Y + 15 + j, zdev(3, 0))
-
-    relay()
+    def relay(j):
+        cols = pl.ds(j * NC, NC)
+        arrived(yrecv.at[0, j], S_Y + j, zdev(1, 0))
+        ysend[4, j] = (yp[yrow(cr, 0), cols] + yrecv[0, j].astype(F32)).astype(BF)
+        send(ysend.at[4, j], yrecv.at[4, j], S_Y + 12 + j, zdev(1, 0))
+        arrived(yrecv.at[1, j], S_Y + 3 + j, zdev(3, 0))
+        ysend[5, j] = (yp[yrow(cl, 1), cols] + yrecv[1, j].astype(F32)).astype(BF)
+        send(ysend.at[5, j], yrecv.at[5, j], S_Y + 15 + j, zdev(3, 0))
 
     for pair in ((2, 1), (3, 0)):
         ya, yb = lax.rem(y + pair[0], 4), lax.rem(y + pair[1], 4)
@@ -207,10 +232,17 @@
             cs[i] = gw[2 * i + 1 - k].astype(BF)
             send(cs.at[i], crecv.at[i], S_CS + i, sib)
 
-    for i in (2, 1, 3):
+    def along_y(i):
         arrived(crecv.at[i], S_CS + i, sib)
         ws[i - 1] = (gw[2 * i + k] + crecv[i].astype(F32)).astype(BF)
         send(ws.at[i - 1], wrecv.at[i - 1], S_WS + i - 1, ydev(i))
+
+    along_y(2)
+    along_y(1)
+    relay(0)
+    along_y(3)
+    relay(1)
+    relay(2)
     arrived(crecv.at[0], S_CS + 0, sib)
 
     for i in (1, 3, 2):
@@ -220,9 +252,9 @@
     sx[...] = total.astype(BF)
     for q in range(4):
         t0 = sx[pl.ds(q * M1, H), pl.ds(128, 128)].astype(F32)
-        t1 = pltpu.roll(sx[pl.ds(q * M1 + H, H), pl.ds(128, 128)].astype(F32), 64, 1)
-        srem[2 * q] = jnp.where(left, t0, t1).astype(BF)
-        srem[2 * q + 1] = jnp.where(left, t1, t0).astype(BF)
+        t1 = swap(sx[pl.ds(q * M1 + H, H), pl.ds(128, 128)].astype(F32))
+        srem[2 * q] = jnp.where(left_h, t0, t1).astype(BF)
+        srem[2 * q + 1] = jnp.where(left_h, t1, t0).astype(BF)
     for dc, dl in offs:
         cc, ll = lax.rem(c + dc, 4), lax.rem(l + dl, 2)
         o = 2 * dc + dl
@@ -254,38 +286,44 @@
         o = 2 * dc + dl
         arrived(fm.at[2 * cc + ll], S_GM + o, zdev(dc, dl))
         arrived(fr.at[2 * cc + ll], S_GR + o, zdev(dc, dl))
-    for q in range(4):
-        gm_out[q] = (fm[2 * q].astype(F32) + fm[2 * q + 1].astype(F32)).astype(BF)
-        gr_out[q] = (fr[2 * q].astype(F32) + fr[2 * q + 1].astype(F32)).astype(BF)
+
+    def unpack(lv):
+        units = []
+        for t in range(4):
+            m = fm[2 * t].astype(F32) + fm[2 * t + 1].astype(F32)
+            p = fr[2 * t].astype(F32) + fr[2 * t + 1].astype(F32)
+            halves = [swap(p), p] if lv else [p, swap(p)]
+            rem = (jnp.concatenate(halves, axis=0), jnp.concatenate(halves[::-1], axis=0))
+            main = [(m, swap(m)), (swap(m), m)]
+            units += [rem] + main if lv else main + [rem]
+        for q in range(6):
+            ga_out[:, 128 * q : 128 * q + 128] = jnp.where(
+                left, units[2 * q][0], units[2 * q + 1][1]
+            ).astype(BF)
+
+    for lv in (0, 1):
+        pl.when(l == lv)(lambda lv=lv: unpack(lv))
 
     for cp in pending:
         cp.wait_send()
 
 
 def per_device(acts, w_out, grad_out):
-    odd = lax.rem(lax.axis_index("row"), 2) == 1
-    a3 = acts.reshape(M1, 4, KB).transpose(1, 0, 2)
-    main = jnp.where(odd, a3[:, :, 64:], a3[:, :, :128])
-    rem = jnp.where(odd, a3[:, :, :64], a3[:, :, 128:])
-    top, low = rem[:, :H], rem[:, H:]
-    rem = jnp.where(
-        odd, jnp.concatenate([low, top], axis=-1), jnp.concatenate([top, low], axis=-1)
-    )
-
     def vm(shape, dtype=BF):
         return pltpu.VMEM(shape, dtype)
 
-    outputs, gm, gr, w_grad = pl.pallas_call(
+    return pl.pallas_call(
         kernel,
-        out_shape=[
-            jax.ShapeDtypeStruct((M1, N), BF),
-            jax.ShapeDtypeStruct((4, M1, 128), BF),
-            jax.ShapeDtypeStruct((4, H, 128), BF),
-            jax.ShapeDtypeStruct((KB, N), BF),
+        out_shape=[vm((M1, N)), vm((M1, 4 * KB)), vm((KB, N))],
+        in_specs=[
+            pl.BlockSpec(memory_space=pltpu.VMEM),
+            pl.BlockSpec(memory_space=pltpu.HBM),
+            pl.BlockSpec(memory_space=pltpu.HBM),
         ],
-        in_specs=[pl.BlockSpec(memory_space=pltpu.VMEM)] * 4,
-        out_specs=[pl.BlockSpec(memory_space=pltpu.VMEM)] * 4,
+        out_specs=[pl.BlockSpec(memory_space=pltpu.VMEM)] * 3,
         scratch_shapes=[
+            vm((4, M1, 128)),
+            vm((4, H, 128)),
             vm((4, MG, XB)),
             vm((8, H, 128)),
             vm((N, N)),
@@ -310,20 +348,12 @@
             pltpu.SemaphoreType.DMA((4,)),
         ],
         compiler_params=pltpu.CompilerParams(
-            collective_id=0, has_side_effects=True, vmem_limit_bytes=60 * 2**20
+            collective_id=0, has_side_effects=True, vmem_limit_bytes=50 * 2**20
         ),
         cost_estimate=pl.CostEstimate(
             flops=6 * MG * N * N, bytes_accessed=3 * 2**20, transcendentals=0
         ),
-    )(main, rem, w_out, grad_out)
-
-    a, b = gr[:, :, :64], gr[:, :, 64:]
-    rem = jnp.where(odd, jnp.concatenate([b, a], axis=1), jnp.concatenate([a, b], axis=1))
-    a3 = jnp.where(
-        odd, jnp.concatenate([rem, gm], axis=-1), jnp.concatenate([gm, rem], axis=-1)
-    )
-    grad_acts = a3.transpose(1, 0, 2).reshape(M1, 4 * KB)
-    return outputs, grad_acts, w_grad
+    )(acts, w_out, grad_out)
 
 
 def solution(mesh):

time: 125 us -> 106 us (0.85)
  Pallas kernels: 115 us -> 99.7 us
  other arithmetic: 1.82 us -> 0 us
    pallas_call x1, Pallas kernels: 115 us -> 99.7 us  [per_device(): pl.pallas_call(kernel, out_shape=[vm((M1, N)), vm((M1, 4 * KB)), vm((KB,...]
    unnamed x8 -> x9, local copies, waits for them, and re-layouts: 2.91 us -> 5.32 us
    reshape x3 -> x0, local copies, waits for them, and re-layouts: 2.27 us -> none  [the longest x2 1.29 us: per_device(): a3 = acts.reshape(M1, 4, KB).transpose(1, 0, 2)]
    select_n x4 -> x0, other arithmetic: 1.61 us -> none  [the longest x1 0.78 us: per_device(): main = jnp.where(odd, a3[:, :, 64:], a3[:, :, :128])]
where the time goes in v3:
time: 106 us
  Pallas kernels  99.7 us (94%)
  local copies, waits for them, and re-layouts  5.32 us (5%)
    pallas_call x1, Pallas kernels, per_device(): pl.pallas_call(kernel, out_shape=[vm((M1, N)), vm((M1, 4 * KB)), vm((KB,...  99.7 us
    unnamed x9, local copies, waits for them, and re-layouts  5.32 us

profile of v3, /device:TPU:1, one launch (start us, length us, event | category | flops | bytes accessed | tf_op | source)
XLA Modules:
  0.0 105.7 jit_solution(9668575974193115389)
XLA Ops:
  0.6 0.0 copy-start
  0.6 1.1 copy-done
  1.7 0.0 copy-start.1
  1.7 1.0 copy-done.1
  2.7 0.0 copy-start.2
  2.7 0.9 copy-done.2
  3.7 99.7 %shard_map.58 = (bf16[160,1536]{1,0:T(8,128)(2,1)S(1)}, bf16[160,768]{1,0:T(8,128)(2,1)S(1)}, bf16[192,1536]{1,0:T(8,128)(2,1)S(1)}) custom-call(bf16[160,768]{1,0:T(8,128)(2,1)S(1)} %copy-done.2, bf16[192,1536]{1,0:T(8,128)(2,1)S(1)} %copy-done, bf16[160,1536]{1,0:T(8,128)(2,1)S(1)} %copy-done.1), custom_call_target="tpu_custom_call" | custom-call | flops 9059696640 | bytes 3145728 | tf_op jit(solution)/shard_map/pallas_call | solution.py:315
  103.4 0.8 copy.9
  104.2 0.7 copy.10
  104.9 0.8 copy.11
Async XLA Ops:
  0.6 1.1 %copy-start = (bf16[192,1536]{1,0:T(8,128)(2,1)S(1)}, bf16[192,1536]{1,0:T(8,128)(2,1)}, u32[]{:S(2)}) copy-start(bf16[192,1536]{1,0:T(8,128)(2,1)} %w_in.1) | copy-start | bytes 1769476
  1.7 1.0 copy-start.1
  2.7 0.9 copy-start.2

commit v4 on v3

--- a/solution.py
+++ b/solution.py
@@ -19,15 +19,15 @@
 NJ = N // NC
 
 S_AM, S_AR, S_AX, S_WY, S_WC, S_G, S_Y, S_GX, S_GM, S_GR, S_CS, S_WS = (
-    0, 8, 16, 19, 22, 26, 32, 50, 53, 61, 69, 73,
+    0, 8, 16, 28, 34, 41, 47, 65, 68, 76, 84, 88,
 )
-N_SEM = 76
+N_SEM = 91
 
 
 def kernel(
-    acts, w_in, g_in,
+    acts_in, w_in, g_in,
     y_out, ga_out, w_out,
-    am_in, ar_in, a4, arb, wb, gb, at4, yp, ysend, yrecv, gs, grecv, sx, srem, fm, fr,
+    acts, am_in, a4, arm, wb, gb, at4, yp, ysend, yrecv, gs, grecv, sz, fz,
     gw, cs, crecv, ws, wrecv, ss, rs, ls,
 ):
     d, r, c = lax.axis_index("depth"), lax.axis_index("row"), lax.axis_index("col")
@@ -46,12 +46,13 @@
     sib = (2 * y + 1 - k, r, c)
     offs = [(dc, dl) for dc in (2, 1, 3, 0) for dl in (0, 1) if (dc, dl) != (0, 0)]
 
+    load = pltpu.make_async_copy(acts_in, acts, ls.at[3])
+    load.start()
     bar = pltpu.get_barrier_semaphore()
     peers = [zdev(*o) for o in offs] + [xdev(i) for i in (1, 2, 3)]
     peers += [ydev(i) for i in (1, 2, 3)] + [sib]
     for p in peers:
         pl.semaphore_signal(bar, inc=1, device_id=p, device_id_type=MESH)
-    pl.semaphore_wait(bar, len(peers))
 
     pending = []
 
@@ -71,9 +72,6 @@
     def rows(i, size):
         return pl.ds(pl.multiple_of(i * size, 16), size)
 
-    def main_lane(q):
-        return pl.ds(pl.multiple_of(q * 256, 128), 128)
-
     lane = lax.broadcasted_iota(jnp.int32, (M1, 128), 1)
     left = lane < 64
     left_h = left[:H]
@@ -88,9 +86,9 @@
         for t in range(4):
             q, odd = divmod(KB * t + 64 * lv, 128)
             if odd:
-                am_in[t] = swap(jnp.where(left, tile(q + 1), tile(q))).astype(BF)
+                am_in[t, :M1] = swap(jnp.where(left, tile(q + 1), tile(q))).astype(BF)
             else:
-                am_in[t] = acts[:, 128 * q : 128 * q + 128]
+                am_in[t, :M1] = acts[:, 128 * q : 128 * q + 128]
             q, odd = divmod(KB * t + 128 * (1 - lv), 128)
             first, second = tile(q)[:H], tile(q)[H:]
             if lv:
@@ -99,16 +97,17 @@
                 first = swap(first)
             else:
                 second = swap(second)
-            ar_in[t] = jnp.where(left_h, first, second).astype(BF)
-
+            am_in[t, M1:] = jnp.where(left_h, first, second).astype(BF)
+
+    load.wait()
     for lv in (0, 1):
         pl.when(l == lv)(lambda lv=lv: pack(lv))
+    pl.semaphore_wait(bar, len(peers))
 
     for dc, dl in offs:
         t = lax.rem(c + dc, 4)
         o = 2 * dc + dl
-        send(am_in.at[t], a4.at[x, rows(c, M1), main_lane(l)], S_AM + o, zdev(dc, dl))
-        send(ar_in.at[t], arb.at[2 * c + l], S_AR + o, zdev(dc, dl))
+        send(am_in.at[t], arm.at[2 * c + l], S_AM + o, zdev(dc, dl))
     h0, h1 = pl.ds(0, H), pl.ds(H, H)
 
     def grow(block, half):
@@ -116,36 +115,59 @@
 
     send(g_in.at[h0], gb.at[grow(c, 0)], S_G + 0, zdev(1, 0))
     send(g_in.at[h1], gb.at[grow(c, 1)], S_G + 1, zdev(3, 0))
-    for i in (2, 1, 3):
-        send(w_in, wb.at[rows(d, KB)], S_WY + i - 1, ydev(i))
-    send(w_in, wb.at[rows(d, KB)], S_WC + 0, sib)
+    def wrow(block, half):
+        return pl.ds(pl.multiple_of(block * KB + half * (KB // 2), 16), KB // 2)
+
+    w0, w1 = pl.ds(0, KB // 2), pl.ds(KB // 2, KB // 2)
+    send(w_in.at[w0], wb.at[wrow(d, 0)], S_WY + 0, ydev(1))
+    send(w_in.at[w1], wb.at[wrow(d, 1)], S_WY + 1, ydev(3))
+    send(w_in.at[w1], wb.at[wrow(d, 1)], S_WY + 2, ydev(1))
+    send(w_in.at[w0], wb.at[wrow(d, 0)], S_WY + 3, ydev(3))
+    send(w_in, wb.at[rows(d, KB)], S_WC + 6, sib)
     send(g_in.at[h1], gb.at[grow(c, 1)], S_G + 2, zdev(1, 0))
     send(g_in.at[h0], gb.at[grow(c, 0)], S_G + 3, zdev(3, 0))
 
     own = [
-        pltpu.make_async_copy(am_in.at[c], a4.at[x, rows(c, M1), main_lane(l)], ls.at[0]),
-        pltpu.make_async_copy(ar_in.at[c], arb.at[2 * c + l], ls.at[1]),
-        pltpu.make_async_copy(w_in, wb.at[rows(d, KB)], ls.at[2]),
-        pltpu.make_async_copy(g_in, gb.at[rows(c, M1)], ls.at[3]),
+        pltpu.make_async_copy(am_in.at[c], arm.at[2 * c + l], ls.at[0]),
+        pltpu.make_async_copy(w_in, wb.at[rows(d, KB)], ls.at[1]),
+        pltpu.make_async_copy(g_in, gb.at[rows(c, M1)], ls.at[2]),
     ]
     for cp in own:
         cp.start()
     own[0].wait()
-    own[1].wait()
-
-    for dc, dl in offs:
-        cc, ll = lax.rem(c + 4 - dc, 4), lax.rem(l + dl, 2)
-        o = 2 * dc + dl
-        arrived(a4.at[x, rows(cc, M1), main_lane(ll)], S_AM + o, zdev(dc, dl))
-        arrived(arb.at[2 * cc + ll], S_AR + o, zdev(dc, dl))
-    for q in range(4):
-        p0, p1 = arb[2 * q].astype(F32), arb[2 * q + 1].astype(F32)
+
+    y_l, y_r, y_o = (2 * lax.rem(y + i, 4) + k for i in (3, 1, 2))
+
+    def pass_w(block, half, sem):
+        place = wb.at[wrow(block, half)]
+        arrived(place, S_WY + sem, sib)
+        if sem < 2:
+            send(place, place, S_WY + 4 + sem, ydev(1 + 2 * sem))
+        send(place, place, S_WC + sem, sib)
+
+    pass_w(y_l, 0, 0)
+    pass_w(y_r, 1, 1)
+
+    x_l, x_r, x_o = (lax.rem(x + i, 4) for i in (3, 1, 2))
+    order = (0, 1, 3, 2)
+    for n, step in enumerate(order):
+        q = lax.rem(c + step, 4)
+        dc = (4 - step) % 4
+        for dl in (0, 1):
+            if (dc, dl) != (0, 0):
+                ll = lax.rem(l + dl, 2)
+                o = 2 * dc + dl
+                arrived(arm.at[2 * q + ll], S_AM + o, sib)
+        a4[x, rows(q, M1), 0:128] = arm[2 * q, :M1]
+        a4[x, rows(q, M1), 256:384] = arm[2 * q + 1, :M1]
+        p0, p1 = arm[2 * q, M1:].astype(F32), arm[2 * q + 1, M1:].astype(F32)
         low = jnp.where(left_h, p0, p1)
         high = swap(jnp.where(left_h, p1, p0))
-        a4[x, pl.ds(q * M1, H), pl.ds(128, 128)] = low.astype(BF)
-        a4[x, pl.ds(q * M1 + H, H), pl.ds(128, 128)] = high.astype(BF)
-    for i in (2, 1, 3):
-        send(a4.at[x], a4.at[x], S_AX + i - 1, xdev(i))
+        a4[x, grow(q, 0), pl.ds(128, 128)] = low.astype(BF)
+        a4[x, grow(q, 1), pl.ds(128, 128)] = high.astype(BF)
+        place = a4.at[x, rows(q, M1)]
+        send(place, place, S_AX + n, xdev(1))
+        send(place, place, S_AX + 4 + n, xdev(3))
 
     cl, cr, co = lax.rem(c + 3, 4), lax.rem(c + 1, 4), lax.rem(c + 2, 4)
     arrived(gb.at[grow(cl, 0)], S_G + 0, zdev(1, 0))
@@ -153,19 +175,35 @@
     arrived(gb.at[grow(cr, 1)], S_G + 1, zdev(3, 0))
     send(gb.at[grow(cr, 1)], gb.at[grow(cr, 1)], S_G + 5, zdev(3, 0))
 
+    pass_w(y_l, 1, 2)
+    pass_w(y_r, 0, 3)
+
+    own[1].wait()
     own[2].wait()
-    own[3].wait()
-    for i in (1, 3, 2):
-        src = 2 * lax.rem(y + 4 - i, 4) + k
-        arrived(wb.at[rows(src, KB)], S_WY + i - 1, ydev(i))
-        send(wb.at[rows(src, KB)], wb.at[rows(src, KB)], S_WC + i, sib)
-
-    for i in (1, 3, 2):
-        src = lax.rem(x + 4 - i, 4)
-        arrived(a4.at[src], S_AX + i - 1, xdev(i))
-    for i in (0, 1, 3, 2):
-        src = 2 * lax.rem(y + 4 - i, 4) + 1 - k
-        arrived(wb.at[rows(src, KB)], S_WC + i, sib)
+
+    def a_rows(xs, n):
+        return a4.at[xs, rows(lax.rem(c + order[n], 4), M1)]
+
+    for n in (0, 2, 1, 3):
+        xs, sem, to = (x_l, n, 1) if n < 2 else (x_r, 4 + n, 3)
+        place = a_rows(xs, n)
+        arrived(place, S_AX + sem, sib)
+        send(place, place, S_AX + 8 + n, xdev(to))
+
+    pass_w(y_o, 0, 4)
+    pass_w(y_o, 1, 5)
+
+    for n in range(4):
+        xs, sem = (x_r, 4 + n) if n < 2 else (x_l, n)
+        arrived(a_rows(xs, n), S_AX + sem, sib)
+    for n in range(4):
+        arrived(a_rows(x_o, n), S_AX + 8 + n, sib)
+    arrived(wb.at[rows(2 * y + 1 - k, KB)], S_WC + 6, sib)
+    flip = 1 - 2 * k
+    for sem, (block, half) in enumerate(
+        ((y_l, 0), (y_r, 1), (y_l, 1), (y_r, 0), (y_o, 0), (y_o, 1))
+    ):
+        arrived(wb.at[wrow(block + flip, half)], S_WC + sem, sib)
 
     def yrow(block, half):
         return pl.ds(pl.multiple_of(block * M1 + half * H, 16), H)
@@ -178,9 +216,8 @@
             yp[:, cols] = jnp.dot(a, wb[:, cols], preferred_element_type=F32)
 
         cols = pl.ds(j * NC, NC)
-        for kind, block, half, dc in ((0, co, 0, 1), (1, co, 1, 3), (2, cr, 1, 1), (3, cl, 0, 3)):
+        for kind, block, half in ((0, co, 0), (1, co, 1), (2, cr, 1), (3, cl, 0)):
             ysend[kind, j] = yp[yrow(block, half), cols].astype(BF)
-            send(ysend.at[kind, j], yrecv.at[kind, j], S_Y + 3 * kind + j, zdev(dc, 0))
 
     for q in range(4):
         at4[q] = a4[q].T
@@ -189,6 +226,14 @@
     arrived(gb.at[grow(cr, 0)], S_G + 3, zdev(3, 0))
     arrived(gb.at[grow(co, 0)], S_G + 4, zdev(1, 0))
     arrived(gb.at[grow(co, 1)], S_G + 5, zdev(3, 0))
+
+    def send_y(first):
+        for j in range(NJ):
+            for kind, dc in ((first, 1), (first + 1, 3)):
+                send(ysend.at[kind, j], yrecv.at[kind, j], S_Y + 3 * kind + j, zdev(dc, 0))
+
+    send_y(0)
+    send_y(2)
 
     def nt_dot(a, b):
         return lax.dot_general(a, b, (((1,), (1,)), ((), ())), preferred_element_type=F32)
@@ -249,19 +294,17 @@
         arrived(grecv.at[i - 1], S_GX + i - 1, xdev(i))
     total = gs[0].astype(F32) + grecv[0].astype(F32)
     total += grecv[1].astype(F32) + grecv[2].astype(F32)
-    sx[...] = total.astype(BF)
     for q in range(4):
-        t0 = sx[pl.ds(q * M1, H), pl.ds(128, 128)].astype(F32)
-        t1 = swap(sx[pl.ds(q * M1 + H, H), pl.ds(128, 128)].astype(F32))
-        srem[2 * q] = jnp.where(left_h, t0, t1).astype(BF)
-        srem[2 * q + 1] = jnp.where(left_h, t1, t0).astype(BF)
+        for ll in (0, 1):
+            sz[2 * q + ll, :M1] = total[q * M1 : (q + 1) * M1, 256 * ll : 256 * ll + 128].astype(BF)
+        t0 = total[q * M1 : q * M1 + H, 128:256]
+        t1 = swap(total[q * M1 + H : (q + 1) * M1, 128:256])
+        sz[2 * q, M1:] = jnp.where(left_h, t0, t1).astype(BF)
+        sz[2 * q + 1, M1:] = jnp.where(left_h, t1, t0).astype(BF)
     for dc, dl in offs:
         cc, ll = lax.rem(c + dc, 4), lax.rem(l + dl, 2)
-        o = 2 * dc + dl
-        send(sx.at[rows(cc, M1), main_lane(ll)], fm.at[2 * c + l], S_GM + o, zdev(dc, dl))
-        send(srem.at[2 * cc + ll], fr.at[2 * c + l], S_GR + o, zdev(dc, dl))
-    fm[2 * c + l] = sx[rows(c, M1), main_lane(l)]
-    fr[2 * c + l] = srem[2 * c + l]
+        send(sz.at[2 * cc + ll], fz.at[2 * c + l], S_GM + 2 * dc + dl, zdev(dc, dl))
+    fz[2 * c + l] = sz[2 * c + l]
 
     for j in range(NJ):
         cols = pl.ds(j * NC, NC)
@@ -284,14 +327,13 @@
     for dc, dl in offs:
         cc, ll = lax.rem(c + 4 - dc, 4), lax.rem(l + dl, 2)
         o = 2 * dc + dl
-        arrived(fm.at[2 * cc + ll], S_GM + o, zdev(dc, dl))
-        arrived(fr.at[2 * cc + ll], S_GR + o, zdev(dc, dl))
+        arrived(fz.at[2 * cc + ll], S_GM + o, zdev(dc, dl))
 
     def unpack(lv):
         units = []
         for t in range(4):
-            m = fm[2 * t].astype(F32) + fm[2 * t + 1].astype(F32)
-            p = fr[2 * t].astype(F32) + fr[2 * t + 1].astype(F32)
+            f = fz[2 * t].astype(F32) + fz[2 * t + 1].astype(F32)
+            m, p = f[:M1], f[M1:]
             halves = [swap(p), p] if lv else [p, swap(p)]
             rem = (jnp.concatenate(halves, axis=0), jnp.concatenate(halves[::-1], axis=0))
             main = [(m, swap(m)), (swap(m), m)]
@@ -316,16 +358,16 @@
         kernel,
         out_shape=[vm((M1, N)), vm((M1, 4 * KB)), vm((KB, N))],
         in_specs=[
-            pl.BlockSpec(memory_space=pltpu.VMEM),
+            pl.BlockSpec(memory_space=pltpu.HBM),
             pl.BlockSpec(memory_space=pltpu.HBM),
             pl.BlockSpec(memory_space=pltpu.HBM),
         ],
         out_specs=[pl.BlockSpec(memory_space=pltpu.VMEM)] * 3,
         scratch_shapes=[
-            vm((4, M1, 128)),
-            vm((4, H, 128)),
+            vm((M1, 4 * KB)),
+            vm((4, M1 + H, 128)),
             vm((4, MG, XB)),
-            vm((8, H, 128)),
+            vm((8, M1 + H, 128)),
             vm((N, N)),
             vm((MG, N)),
             vm((4, XB, MG)),
@@ -334,10 +376,8 @@
             vm((6, NJ, H, NC)),
             vm((4, MG, XB)),
             vm((3, MG, XB)),
-            vm((MG, XB)),
-            vm((8, H, 128)),
-            vm((8, M1, 128)),
-            vm((8, H, 128)),
+            vm((8, M1 + H, 128)),
+            vm((8, M1 + H, 128)),
             vm((8, KB, N), F32),
             vm((4, KB, N)),
             vm((4, KB, N)),
@@ -348,7 +388,7 @@
             pltpu.SemaphoreType.DMA((4,)),
         ],
         compiler_params=pltpu.CompilerParams(
-            collective_id=0, has_side_effects=True, vmem_limit_bytes=50 * 2**20
+            collective_id=0, has_side_effects=True, vmem_limit_bytes=62 * 2**20
         ),
         cost_estimate=pl.CostEstimate(
             flops=6 * MG * N * N, bytes_accessed=3 * 2**20, transcendentals=0

time: 106 us -> 101 us (0.953)
  local copies, waits for them, and re-layouts: 5.32 us -> 2.29 us
  Pallas kernels: 99.7 us -> 97.7 us
    unnamed x9 -> x3, local copies, waits for them, and re-layouts: 5.32 us -> 2.29 us
    pallas_call x1, Pallas kernels: 99.7 us -> 97.7 us  [per_device(): pl.pallas_call(kernel, out_shape=[vm((M1, N)), vm((M1, 4 * KB)), vm((KB,...]
where the time goes in v4:
time: 101 us
  Pallas kernels  97.7 us (97%)
  local copies, waits for them, and re-layouts  2.29 us (2%)
    pallas_call x1, Pallas kernels, per_device(): pl.pallas_call(kernel, out_shape=[vm((M1, N)), vm((M1, 4 * KB)), vm((KB,...  97.7 us
    unnamed x3, local copies, waits for them, and re-layouts  2.29 us

profile of v4, /device:TPU:1, one launch (start us, length us, event | category | flops | bytes accessed | tf_op | source)
XLA Modules:
  0.0 100.6 jit_solution(2234591193314272557)
XLA Ops:
  0.6 97.7 %shard_map.58 = (bf16[160,1536]{1,0:T(8,128)(2,1)S(1)}, bf16[160,768]{1,0:T(8,128)(2,1)S(1)}, bf16[192,1536]{1,0:T(8,128)(2,1)S(1)}) custom-call(bf16[160,768]{1,0:T(8,128)(2,1)} %acts_in.1, bf16[192,1536]{1,0:T(8,128)(2,1)} %w_in.1, bf16[160,1536]{1,0:T(8,128)(2,1)} %g_in.1), custom_call_target="tpu_custom_call" | custom-call | flops 9059696640 | bytes 3145728 | tf_op jit(solution)/shard_map/pallas_call | solution.py:357
  98.3 0.8 copy.9
  99.1 0.7 copy.10
  99.8 0.8 copy.11

commit v5 on v4

--- a/solution.py
+++ b/solution.py
@@ -233,7 +233,6 @@
                 send(ysend.at[kind, j], yrecv.at[kind, j], S_Y + 3 * kind + j, zdev(dc, 0))
 
     send_y(0)
-    send_y(2)
 
     def nt_dot(a, b):
         return lax.dot_general(a, b, (((1,), (1,)), ((), ())), preferred_element_type=F32)
@@ -253,6 +252,8 @@
             if i:
                 send(gs.at[i], grecv.at[i - 1], S_GX + i - 1, xdev(i))
 
+    send_y(2)
+
     def relay(j):
         cols = pl.ds(j * NC, NC)
         arrived(yrecv.at[0, j], S_Y + j, zdev(1, 0))
@@ -283,11 +284,11 @@
         send(ws.at[i - 1], wrecv.at[i - 1], S_WS + i - 1, ydev(i))
 
     along_y(2)
-    along_y(1)
     relay(0)
-    along_y(3)
     relay(1)
     relay(2)
+    along_y(1)
+    along_y(3)
     arrived(crecv.at[0], S_CS + 0, sib)
 
     for i in (1, 3, 2):

time: 101 us -> 101 us (level)
  no operation moved by 1% of the time
where the time goes in v5:
time: 101 us
  Pallas kernels  97.7 us (97%)
  local copies, waits for them, and re-layouts  2.29 us (2%)
    pallas_call x1, Pallas kernels, per_device(): pl.pallas_call(kernel, out_shape=[vm((M1, N)), vm((M1, 4 * KB)), vm((KB,...  97.7 us
    unnamed x3, local copies, waits for them, and re-layouts  2.29 us

profile of v5, /device:TPU:1, one launch (start us, length us, event | category | flops | bytes accessed | tf_op | source)
XLA Modules:
  0.0 100.6 jit_solution(8036728035635940278)
XLA Ops:
  0.6 97.7 %shard_map.58 = (bf16[160,1536]{1,0:T(8,128)(2,1)S(1)}, bf16[160,768]{1,0:T(8,128)(2,1)S(1)}, bf16[192,1536]{1,0:T(8,128)(2,1)S(1)}) custom-call(bf16[160,768]{1,0:T(8,128)(2,1)} %acts_in.1, bf16[192,1536]{1,0:T(8,128)(2,1)} %w_in.1, bf16[160,1536]{1,0:T(8,128)(2,1)} %g_in.1), custom_call_target="tpu_custom_call" | custom-call | flops 9059696640 | bytes 3145728 | tf_op jit(solution)/shard_map/pallas_call | solution.py:358
  98.3 0.8 copy.9
  99.1 0.7 copy.10
  99.8 0.8 copy.11
